TPU v7x, 512 devices: a whole 4x8x8 slice. The times are simulated.
512 devices in a mesh: tm: 256 (over z, y, x), col: 2 (over core).
Axes of the slice: x: 4, y: 8, z: 8, core: 2. Of those that a mesh axis runs over, the one named last changes fastest.
Arguments:
- observations: float32 [1, 256, 256], P(None, 'tm'), may hold values from -6 to 6
- sensor_mask: int32 [1, 256, 256], P(None, 'tm'), may hold values 0 or 1
- filter_gain: float32 [1, 256, 256, 256], P(None, 'tm', 'col'), may hold values from -1 to 1
- smoother_gain: float32 [1, 256, 256, 256], P(None, 'tm', 'col'), may hold values from -1 to 1
- dynamics: float32 [1, 256, 256], replicated, may hold values from -1 to 1
- process_noise: float32 [1, 256, 256], replicated, may hold values from -1 to 1, as said below
- sensor_noise: float32 [1, 256], replicated, may hold values from 0.1 to 4
- initial_mean: float32 [1, 256], replicated, may hold values from -6 to 6
- initial_cov: float32 [1, 256, 256], replicated, may hold values from -2 to 3, as said below
Outputs:
- smoothed_mean: float32 [1, 256, 256], P(None, 'tm', 'col')
- smoothed_cov: float32 [1, 256, 256, 256], P(None, 'tm', 'col')
Inputs may be any that keep to these rules, and one draw needn't show every extreme that they name: `process_noise`: symmetric. `initial_cov`: symmetric.
All inputs are finite; a program needn't handle non-finite values. No bound on the sum of `sensor_mask` on one device may be relied on, other than what follows from the above.
Results may differ from a plain program's by a relative error of at most 0.0003.
Values sent between devices are 32-bit elements; how exact they have to be, the bound alone decides.
A program may use at most 64 MiB of HBM per device.

v0:
```python
import jax
import jax.numpy as jnp
from jax import lax
from jax.sharding import PartitionSpec as P


def shifted(value, axis, by):
    count = lax.axis_size(axis)
    pairs = [(i, i + by) for i in range(count) if 0 <= i + by < count]
    return lax.ppermute(value, axis, pairs)


def product(left, right):
    return jnp.matmul(left, right, precision=lax.Precision.HIGHEST)


def combine(earlier, later):
    head_map, head_shift, head_cov = earlier
    tail_map, tail_shift, tail_cov = later
    full_map, full_shift, full_cov, tail_full = (
        lax.all_gather(head_map, "col", axis=1, tiled=True),
        lax.all_gather(head_shift, "col", axis=1, tiled=True),
        lax.all_gather(head_cov, "col", axis=1, tiled=True),
        lax.all_gather(tail_map, "col", axis=1, tiled=True),
    )
    new_map = product(tail_map, full_map)
    new_shift = (
        jnp.einsum("brn,bn->br", tail_map, full_shift, precision=lax.Precision.HIGHEST) + tail_shift
    )
    new_cov = product(product(tail_map, full_cov), jnp.swapaxes(tail_full, 1, 2)) + tail_cov
    return (new_map, new_shift, new_cov)


def passed(element, stride):
    return shifted(element, "tm", stride)


def run_scan(maps, shifts, covs, reverse):
    steps = maps.shape[1]
    order = list(range(steps))
    if reverse:
        order = order[::-1]
    prefix = [None] * steps
    prefix[order[0]] = (maps[:, order[0]], shifts[:, order[0]], covs[:, order[0]])
    total = prefix[order[-1]]
    devices = lax.axis_size("tm")
    place = lax.axis_index("tm")
    stride = 1
    while stride < devices:
        moved = passed(total, -stride if reverse else stride)
        merged = combine(moved, total)
        valid = place < devices - stride if reverse else place >= stride
        total = tuple((jnp.where(valid, fresh, stale) for fresh, stale in zip(merged, total)))
        stride = stride * 2
    carry_map, carry_shift, carry_cov = passed(total, -1 if reverse else 1)
    prefix_map = jnp.stack([item[0] for item in prefix], 1)
    prefix_shift = jnp.stack([item[1] for item in prefix], 1)
    prefix_cov = jnp.stack([item[2] for item in prefix], 1)
    full_map, full_shift, full_cov, carry_shift, carry_cov = (
        lax.all_gather(prefix_map, "col", axis=2, tiled=True),
        lax.all_gather(prefix_shift, "col", axis=2, tiled=True),
        lax.all_gather(prefix_cov, "col", axis=2, tiled=True),
        lax.all_gather(carry_shift[:, None], "col", axis=2, tiled=True),
        lax.all_gather(carry_cov[:, None], "col", axis=2, tiled=True),
    )
    carry_shift = carry_shift[:, 0]
    carry_cov = carry_cov[:, 0]
    mean = (
        jnp.einsum("bsrn,bn->bsr", full_map, carry_shift, precision=lax.Precision.HIGHEST)
        + full_shift
    )
    cov = product(product(full_map, carry_cov[:, None]), jnp.swapaxes(full_map, 2, 3)) + full_cov
    return (mean, cov)


def shards(
    observations,
    sensor_mask,
    filter_gain,
    smoother_gain,
    dynamics,
    process_noise,
    sensor_noise,
    initial_mean,
    initial_cov,
):
    steps = filter_gain.shape[1]
    rows_dev = filter_gain.shape[2]
    state = filter_gain.shape[3]
    start_row = lax.axis_index("col") * rows_dev
    weight = sensor_mask.astype(jnp.float32)
    gain_rows = filter_gain * weight[:, :, None, :]
    gain_whole, smooth_full = (
        lax.all_gather(filter_gain, "col", axis=2, tiled=True),
        lax.all_gather(smoother_gain, "col", axis=2, tiled=True),
    )
    gain_full = gain_whole * weight[:, :, None, :]
    identity = jnp.eye(state, dtype=jnp.float32)
    gain_own, smooth_own = (gain_rows, smoother_gain)
    eye_own = lax.dynamic_slice_in_dim(identity, start_row, rows_dev, 0)

    def own_rows(values, axis):
        return lax.dynamic_slice_in_dim(values, start_row, rows_dev, axis)

    keep_full = identity - gain_full
    keep_own = eye_own - gain_own
    step_map = product(keep_own, dynamics[:, None])
    step_shift = jnp.einsum(
        "bsrn,bsn->bsr", gain_own, observations, precision=lax.Precision.HIGHEST
    )
    step_cov = product(product(keep_own, process_noise[:, None]), jnp.swapaxes(keep_full, 2, 3))
    step_cov = step_cov + product(
        gain_own * sensor_noise[:, None, None, :], jnp.swapaxes(gain_full, 2, 3)
    )
    opening_full = product(keep_full[:, 0], dynamics)
    opening_shift = (
        jnp.einsum("brn,bn->br", step_map[:, 0], initial_mean, precision=lax.Precision.HIGHEST)
        + step_shift[:, 0]
    )
    opening_cov = (
        product(product(step_map[:, 0], initial_cov), jnp.swapaxes(opening_full, 1, 2))
        + step_cov[:, 0]
    )
    opening = (lax.axis_index("tm") == 0) & (jnp.arange(steps) == 0)
    step_map = jnp.where(opening[None, :, None, None], 0.0, step_map)
    step_shift = jnp.where(opening[None, :, None], opening_shift[:, None], step_shift)
    step_cov = jnp.where(opening[None, :, None, None], opening_cov[:, None], step_cov)
    filt_mean, filt_cov = run_scan(step_map, step_shift, step_cov, False)
    predicted = (
        product(product(dynamics[:, None], filt_cov), jnp.swapaxes(dynamics, 1, 2)[:, None])
        + process_noise[:, None]
    )
    moved_mean = jnp.einsum("bmn,bsn->bsm", dynamics, filt_mean, precision=lax.Precision.HIGHEST)
    own_mean = own_rows(filt_mean, 2)
    own_cov = own_rows(filt_cov, 2)
    back_shift = own_mean - jnp.einsum(
        "bsrn,bsn->bsr", smooth_own, moved_mean, precision=lax.Precision.HIGHEST
    )
    back_cov = own_cov - product(product(smooth_own, predicted), jnp.swapaxes(smooth_full, 2, 3))
    closing = (lax.axis_index("tm") == lax.axis_size("tm") - 1) & (jnp.arange(steps) == steps - 1)
    back_map = jnp.where(closing[None, :, None, None], 0.0, smooth_own)
    back_shift = jnp.where(closing[None, :, None], own_mean, back_shift)
    back_cov = jnp.where(closing[None, :, None, None], own_cov, back_cov)
    smooth_mean, smooth_cov = run_scan(back_map, back_shift, back_cov, True)
    smoothed_mean = lax.dynamic_slice_in_dim(smooth_mean, start_row, rows_dev, 2)
    smoothed_cov = lax.dynamic_slice_in_dim(smooth_cov, start_row, rows_dev, 2)
    return (smoothed_mean, smoothed_cov)


def solution(mesh):
    return jax.shard_map(
        shards,
        mesh=mesh,
        in_specs=(
            P(None, "tm", None),
            P(None, "tm", None),
            P(None, "tm", "col", None),
            P(None, "tm", "col", None),
            P(),
            P(),
            P(),
            P(),
            P(),
        ),
        out_specs=(P(None, "tm", "col"), P(None, "tm", "col", None)),
        check_vma=False,
    )
```

profile of v0, /device:TPU:1, one launch (start us, length us, event | category | flops | bytes accessed | tf_op | source)
XLA Modules:
  0.0 391.6 jit_solution(12741671661961222988)
XLA Ops:
  3.4 4.0 %collective-permute-start.14 = (f32[1,128]{1,0:T(1,128)S(1)}, f32[1,128]{1,0:T(1,128)S(1)}, u32[]{:S(2)}, u32[]{:S(2)}) collective-permute-start(f32[1,128]{1,0:T(1,128)S(1)} %bitcast.700), channel_id=1, source_target_pairs={{0,2},{2,4},{4,6},{6,8},{8,10},{10,12},{12,14},{14,16},{16,18},{18... | collective-permute-start | bytes 1544 | tf_op jit(solution)/shard_map/ppermute | solution.py:10
  12.0 4.0 %all_gather.258 = f32[1,1,256,256]{3,2,1,0:T(8,128)S(1)} all-gather(f32[1,1,128,256]{3,2,1,0:T(8,128)S(1)} %copy-done.1), channel_id=1, replica_groups=mesh['tm'=256,'col'=2] {'col'}, dimensions={2}, use_global_device_ids=true | all-gather | bytes 393216 | tf_op jit(solution)/shard_map/all_gather | solution.py:94
  19.5 4.3 %collective-permute-start.32 = (f32[1,128,256]{2,1,0:T(8,128)S(1)}, f32[1,128,256]{2,1,0:T(8,128)S(1)}, u32[]{:S(2)}, u32[]{:S(2)}) collective-permute-start(f32[1,128,256]{2,1,0:T(8,128)S(1)} %bitcast.676), channel_id=1, source_target_pairs={{0,2},{2,4},{4,6},{6,8},{8,10},{10,12},{12,14},{14,16},{16,18},{18... | collective-permute-start | bytes 393224 | tf_op jit(solution)/shard_map/ppermute | solution.py:10
  34.0 3.2 collective-permute-start.15
  43.3 4.9 %collective-permute-start.8 = (f32[1,128,256]{2,1,0:T(8,128)S(1)}, f32[1,128,256]{2,1,0:T(8,128)S(1)}, u32[]{:S(2)}, u32[]{:S(2)}) collective-permute-start(f32[1,128,256]{2,1,0:T(8,128)S(1)} %bitcast.669), channel_id=1, source_target_pairs={{0,4},{2,6},{4,8},{6,10},{8,12},{10,14},{12,16},{14,18},{16,20},{1... | collective-permute-start | bytes 393224 | tf_op jit(solution)/shard_map/ppermute | solution.py:10
  48.4 3.2 collective-permute-start.16
  62.4 5.8 %collective-permute-start.33 = (f32[1,128,256]{2,1,0:T(8,128)S(1)}, f32[1,128,256]{2,1,0:T(8,128)S(1)}, u32[]{:S(2)}, u32[]{:S(2)}) collective-permute-start(f32[1,128,256]{2,1,0:T(8,128)S(1)} %bitcast.680), channel_id=1, source_target_pairs={{0,4},{2,6},{4,8},{6,10},{8,12},{10,14},{12,16},{14,18},{16,20},{1... | collective-permute-start | bytes 393224 | tf_op jit(solution)/shard_map/ppermute | solution.py:10
  76.0 7.6 %collective-permute-start.17 = (f32[1,128]{1,0:T(1,128)S(1)}, f32[1,128]{1,0:T(1,128)S(1)}, u32[]{:S(2)}, u32[]{:S(2)}) collective-permute-start(f32[1,128]{1,0:T(1,128)S(1)} %bitcast.703), channel_id=1, source_target_pairs={{0,16},{2,18},{4,20},{6,22},{8,24},{10,26},{12,28},{14,30},{16,32}... | collective-permute-start | bytes 1544 | tf_op jit(solution)/shard_map/ppermute | solution.py:10
  94.3 4.3 %collective-permute-start.34 = (f32[1,128,256]{2,1,0:T(8,128)S(1)}, f32[1,128,256]{2,1,0:T(8,128)S(1)}, u32[]{:S(2)}, u32[]{:S(2)}) collective-permute-start(f32[1,128,256]{2,1,0:T(8,128)S(1)} %bitcast.678), channel_id=1, source_target_pairs={{0,8},{2,10},{4,12},{6,14},{8,16},{10,18},{12,20},{14,22},{16,24},... | collective-permute-start | bytes 393224 | tf_op jit(solution)/shard_map/ppermute | solution.py:10
  106.2 5.7 %collective-permute-start.18 = (f32[1,128]{1,0:T(1,128)S(1)}, f32[1,128]{1,0:T(1,128)S(1)}, u32[]{:S(2)}, u32[]{:S(2)}) collective-permute-start(f32[1,128]{1,0:T(1,128)S(1)} %bitcast.704), channel_id=1, source_target_pairs={{0,32},{2,34},{4,36},{6,38},{8,40},{10,42},{12,44},{14,46},{16,48}... | collective-permute-start | bytes 1544 | tf_op jit(solution)/shard_map/ppermute | solution.py:10
  122.6 5.8 %collective-permute-start.35 = (f32[1,128,256]{2,1,0:T(8,128)S(1)}, f32[1,128,256]{2,1,0:T(8,128)S(1)}, u32[]{:S(2)}, u32[]{:S(2)}) collective-permute-start(f32[1,128,256]{2,1,0:T(8,128)S(1)} %bitcast.679), channel_id=1, source_target_pairs={{0,16},{2,18},{4,20},{6,22},{8,24},{10,26},{12,28},{14,30},{16,32}... | collective-permute-start | bytes 393224 | tf_op jit(solution)/shard_map/ppermute | solution.py:10
  132.8 5.2 %collective-permute-start.11 = (f32[1,128,256]{2,1,0:T(8,128)S(1)}, f32[1,128,256]{2,1,0:T(8,128)S(1)}, u32[]{:S(2)}, u32[]{:S(2)}) collective-permute-start(f32[1,128,256]{2,1,0:T(8,128)S(1)} %bitcast.672), channel_id=1, source_target_pairs={{0,32},{2,34},{4,36},{6,38},{8,40},{10,42},{12,44},{14,46},{16,48}... | collective-permute-start | bytes 393224 | tf_op jit(solution)/shard_map/ppermute | solution.py:10
  138.2 4.0 %collective-permute-start.19 = (f32[1,128]{1,0:T(1,128)S(1)}, f32[1,128]{1,0:T(1,128)S(1)}, u32[]{:S(2)}, u32[]{:S(2)}) collective-permute-start(f32[1,128]{1,0:T(1,128)S(1)} %bitcast.705), channel_id=1, source_target_pairs={{0,64},{2,66},{4,68},{6,70},{8,72},{10,74},{12,76},{14,78},{16,80}... | collective-permute-start | bytes 1544 | tf_op jit(solution)/shard_map/ppermute | solution.py:10
  153.0 8.2 %collective-permute-start.36 = (f32[1,128,256]{2,1,0:T(8,128)S(1)}, f32[1,128,256]{2,1,0:T(8,128)S(1)}, u32[]{:S(2)}, u32[]{:S(2)}) collective-permute-start(f32[1,128,256]{2,1,0:T(8,128)S(1)} %bitcast.682), channel_id=1, source_target_pairs={{0,32},{2,34},{4,36},{6,38},{8,40},{10,42},{12,44},{14,46},{16,48}... | collective-permute-start | bytes 393224 | tf_op jit(solution)/shard_map/ppermute | solution.py:10
  165.6 8.4 %collective-permute-start.12 = (f32[1,128,256]{2,1,0:T(8,128)S(1)}, f32[1,128,256]{2,1,0:T(8,128)S(1)}, u32[]{:S(2)}, u32[]{:S(2)}) collective-permute-start(f32[1,128,256]{2,1,0:T(8,128)S(1)} %bitcast.673), channel_id=1, source_target_pairs={{0,64},{2,66},{4,68},{6,70},{8,72},{10,74},{12,76},{14,78},{16,80}... | collective-permute-start | bytes 393224 | tf_op jit(solution)/shard_map/ppermute | solution.py:10
  174.2 3.8 collective-permute-start.20
  217.6 11.7 %collective-permute-start.39 = (f32[1,128,256]{2,1,0:T(8,128)S(1)}, f32[1,128,256]{2,1,0:T(8,128)S(1)}, u32[]{:S(2)}, u32[]{:S(2)}) collective-permute-start(f32[1,128,256]{2,1,0:T(8,128)S(1)} %bitcast.685), channel_id=1, source_target_pairs={{0,256},{2,258},{4,260},{6,262},{8,264},{10,266},{12,268},{14,270}... | collective-permute-start | bytes 393224 | tf_op jit(solution)/shard_map/ppermute | solution.py:10
  261.7 6.0 %collective-permute-done.26 = f32[1,128]{1,0:T(1,128)S(1)} collective-permute-done((f32[1,128]{1,0:T(1,128)S(1)}, f32[1,128]{1,0:T(1,128)S(1)}, u32[]{:S(2)}, u32[]{:S(2)}) %collective-permute-start.26) | collective-permute-done | bytes 544 | tf_op jit(solution)/shard_map/ppermute | solution.py:10
  276.0 5.4 %collective-permute-done.42 = f32[1,128,256]{2,1,0:T(8,128)S(1)} collective-permute-done((f32[1,128,256]{2,1,0:T(8,128)S(1)}, f32[1,128,256]{2,1,0:T(8,128)S(1)}, u32[]{:S(2)}, u32[]{:S(2)}) %collective-permute-start.42) | collective-permute-done | bytes 131104 | tf_op jit(solution)/shard_map/ppermute | solution.py:10
  301.2 6.1 %collective-permute-done.28 = f32[1,128]{1,0:T(1,128)S(1)} collective-permute-done((f32[1,128]{1,0:T(1,128)S(1)}, f32[1,128]{1,0:T(1,128)S(1)}, u32[]{:S(2)}, u32[]{:S(2)}) %collective-permute-start.28) | collective-permute-done | bytes 544 | tf_op jit(solution)/shard_map/ppermute | solution.py:10
  331.7 4.8 %collective-permute-done.46 = f32[1,128,256]{2,1,0:T(8,128)S(1)} collective-permute-done((f32[1,128,256]{2,1,0:T(8,128)S(1)}, f32[1,128,256]{2,1,0:T(8,128)S(1)}, u32[]{:S(2)}, u32[]{:S(2)}) %collective-permute-start.46) | collective-permute-done | bytes 131104 | tf_op jit(solution)/shard_map/ppermute | solution.py:10
  348.0 3.4 collective-permute-done.47
  351.4 3.5 all_gather.290
  362.8 14.6 %collective-permute-done.48 = f32[1,128,256]{2,1,0:T(8,128)S(1)} collective-permute-done((f32[1,128,256]{2,1,0:T(8,128)S(1)}, f32[1,128,256]{2,1,0:T(8,128)S(1)}, u32[]{:S(2)}, u32[]{:S(2)}) %collective-permute-start.48) | collective-permute-done | bytes 131104 | tf_op jit(solution)/shard_map/ppermute | solution.py:10
  (251 shorter events, 251.8 us)
Async XLA Ops:
  3.4 28.6 %collective-permute-start.14 = (f32[1,128]{1,0:T(1,128)S(1)}, f32[1,128]{1,0:T(1,128)S(1)}, u32[]{:S(2)}, u32[]{:S(2)}) collective-permute-start(f32[1,128]{1,0:T(1,128)S(1)} %bitcast.700), channel_id=1, source_target_pairs={{0,2},{2,4},{4,6},{6,8},{8,10},{10,12},{12,14},{14,16},{16,18},{18... | collective-permute-start | bytes 1544 | tf_op jit(solution)/shard_map/ppermute | solution.py:10
  7.4 33.7 %collective-permute-start.7 = (f32[1,128,256]{2,1,0:T(8,128)S(1)}, f32[1,128,256]{2,1,0:T(8,128)S(1)}, u32[]{:S(2)}, u32[]{:S(2)}) collective-permute-start(f32[1,128,256]{2,1,0:T(8,128)S(1)} %bitcast.668), channel_id=1, source_target_pairs={{0,2},{2,4},{4,6},{6,8},{8,10},{10,12},{12,14},{14,16},{16,18},{18... | collective-permute-start | bytes 393224 | tf_op jit(solution)/shard_map/ppermute | solution.py:10
  10.6 41.1 %collective-permute-start = (f32[1,128,256]{2,1,0:T(8,128)S(1)}, f32[1,128,256]{2,1,0:T(8,128)S(1)}, u32[]{:S(2)}, u32[]{:S(2)}) collective-permute-start(f32[1,128,256]{2,1,0:T(8,128)S(1)} %fusion.265), channel_id=1, source_target_pairs={{2,0},{4,2},{6,4},{8,6},{10,8},{12,10},{14,12},{16,14},{18,16},{20... | collective-permute-start | bytes 393224 | tf_op jit(solution)/shard_map/ppermute | solution.py:10
  19.5 40.2 %collective-permute-start.32 = (f32[1,128,256]{2,1,0:T(8,128)S(1)}, f32[1,128,256]{2,1,0:T(8,128)S(1)}, u32[]{:S(2)}, u32[]{:S(2)}) collective-permute-start(f32[1,128,256]{2,1,0:T(8,128)S(1)} %bitcast.676), channel_id=1, source_target_pairs={{0,2},{2,4},{4,6},{6,8},{8,10},{10,12},{12,14},{14,16},{16,18},{18... | collective-permute-start | bytes 393224 | tf_op jit(solution)/shard_map/ppermute | solution.py:10
  43.3 27.0 %collective-permute-start.8 = (f32[1,128,256]{2,1,0:T(8,128)S(1)}, f32[1,128,256]{2,1,0:T(8,128)S(1)}, u32[]{:S(2)}, u32[]{:S(2)}) collective-permute-start(f32[1,128,256]{2,1,0:T(8,128)S(1)} %bitcast.669), channel_id=1, source_target_pairs={{0,4},{2,6},{4,8},{6,10},{8,12},{10,14},{12,16},{14,18},{16,20},{1... | collective-permute-start | bytes 393224 | tf_op jit(solution)/shard_map/ppermute | solution.py:10
  48.4 19.8 %collective-permute-start.16 = (f32[1,128]{1,0:T(1,128)S(1)}, f32[1,128]{1,0:T(1,128)S(1)}, u32[]{:S(2)}, u32[]{:S(2)}) collective-permute-start(f32[1,128]{1,0:T(1,128)S(1)} %bitcast.702), channel_id=1, source_target_pairs={{0,8},{2,10},{4,12},{6,14},{8,16},{10,18},{12,20},{14,22},{16,24},... | collective-permute-start | bytes 1544 | tf_op jit(solution)/shard_map/ppermute | solution.py:10
  54.4 29.1 %collective-permute-start.1 = (f32[1,128,256]{2,1,0:T(8,128)S(1)}, f32[1,128,256]{2,1,0:T(8,128)S(1)}, u32[]{:S(2)}, u32[]{:S(2)}) collective-permute-start(f32[1,128,256]{2,1,0:T(8,128)S(1)} %bitcast.662), channel_id=1, source_target_pairs={{4,0},{6,2},{8,4},{10,6},{12,8},{14,10},{16,12},{18,14},{20,16},{2... | collective-permute-start | bytes 393224 | tf_op jit(solution)/shard_map/ppermute | solution.py:10
  62.4 29.2 %collective-permute-start.33 = (f32[1,128,256]{2,1,0:T(8,128)S(1)}, f32[1,128,256]{2,1,0:T(8,128)S(1)}, u32[]{:S(2)}, u32[]{:S(2)}) collective-permute-start(f32[1,128,256]{2,1,0:T(8,128)S(1)} %bitcast.680), channel_id=1, source_target_pairs={{0,4},{2,6},{4,8},{6,10},{8,12},{10,14},{12,16},{14,18},{16,20},{1... | collective-permute-start | bytes 393224 | tf_op jit(solution)/shard_map/ppermute | solution.py:10
  72.6 28.1 %collective-permute-start.9 = (f32[1,128,256]{2,1,0:T(8,128)S(1)}, f32[1,128,256]{2,1,0:T(8,128)S(1)}, u32[]{:S(2)}, u32[]{:S(2)}) collective-permute-start(f32[1,128,256]{2,1,0:T(8,128)S(1)} %bitcast.670), channel_id=1, source_target_pairs={{0,8},{2,10},{4,12},{6,14},{8,16},{10,18},{12,20},{14,22},{16,24},... | collective-permute-start | bytes 393224 | tf_op jit(solution)/shard_map/ppermute | solution.py:10
  76.0 22.6 %collective-permute-start.17 = (f32[1,128]{1,0:T(1,128)S(1)}, f32[1,128]{1,0:T(1,128)S(1)}, u32[]{:S(2)}, u32[]{:S(2)}) collective-permute-start(f32[1,128]{1,0:T(1,128)S(1)} %bitcast.703), channel_id=1, source_target_pairs={{0,16},{2,18},{4,20},{6,22},{8,24},{10,26},{12,28},{14,30},{16,32}... | collective-permute-start | bytes 1544 | tf_op jit(solution)/shard_map/ppermute | solution.py:10
  86.3 25.5 %collective-permute-start.2 = (f32[1,128,256]{2,1,0:T(8,128)S(1)}, f32[1,128,256]{2,1,0:T(8,128)S(1)}, u32[]{:S(2)}, u32[]{:S(2)}) collective-permute-start(f32[1,128,256]{2,1,0:T(8,128)S(1)} %bitcast.663), channel_id=1, source_target_pairs={{8,0},{10,2},{12,4},{14,6},{16,8},{18,10},{20,12},{22,14},{24,16},... | collective-permute-start | bytes 393224 | tf_op jit(solution)/shard_map/ppermute | solution.py:10
  94.3 25.6 %collective-permute-start.34 = (f32[1,128,256]{2,1,0:T(8,128)S(1)}, f32[1,128,256]{2,1,0:T(8,128)S(1)}, u32[]{:S(2)}, u32[]{:S(2)}) collective-permute-start(f32[1,128,256]{2,1,0:T(8,128)S(1)} %bitcast.678), channel_id=1, source_target_pairs={{0,8},{2,10},{4,12},{6,14},{8,16},{10,18},{12,20},{14,22},{16,24},... | collective-permute-start | bytes 393224 | tf_op jit(solution)/shard_map/ppermute | solution.py:10
  103.0 27.6 %collective-permute-start.10 = (f32[1,128,256]{2,1,0:T(8,128)S(1)}, f32[1,128,256]{2,1,0:T(8,128)S(1)}, u32[]{:S(2)}, u32[]{:S(2)}) collective-permute-start(f32[1,128,256]{2,1,0:T(8,128)S(1)} %bitcast.671), channel_id=1, source_target_pairs={{0,16},{2,18},{4,20},{6,22},{8,24},{10,26},{12,28},{14,30},{16,32}... | collective-permute-start | bytes 393224 | tf_op jit(solution)/shard_map/ppermute | solution.py:10
  106.2 22.3 %collective-permute-start.18 = (f32[1,128]{1,0:T(1,128)S(1)}, f32[1,128]{1,0:T(1,128)S(1)}, u32[]{:S(2)}, u32[]{:S(2)}) collective-permute-start(f32[1,128]{1,0:T(1,128)S(1)} %bitcast.704), channel_id=1, source_target_pairs={{0,32},{2,34},{4,36},{6,38},{8,40},{10,42},{12,44},{14,46},{16,48}... | collective-permute-start | bytes 1544 | tf_op jit(solution)/shard_map/ppermute | solution.py:10
  114.6 27.6 %collective-permute-start.3 = (f32[1,128,256]{2,1,0:T(8,128)S(1)}, f32[1,128,256]{2,1,0:T(8,128)S(1)}, u32[]{:S(2)}, u32[]{:S(2)}) collective-permute-start(f32[1,128,256]{2,1,0:T(8,128)S(1)} %bitcast.664), channel_id=1, source_target_pairs={{16,0},{18,2},{20,4},{22,6},{24,8},{26,10},{28,12},{30,14},{32,16}... | collective-permute-start | bytes 393224 | tf_op jit(solution)/shard_map/ppermute | solution.py:10
  122.6 27.7 %collective-permute-start.35 = (f32[1,128,256]{2,1,0:T(8,128)S(1)}, f32[1,128,256]{2,1,0:T(8,128)S(1)}, u32[]{:S(2)}, u32[]{:S(2)}) collective-permute-start(f32[1,128,256]{2,1,0:T(8,128)S(1)} %bitcast.679), channel_id=1, source_target_pairs={{0,16},{2,18},{4,20},{6,22},{8,24},{10,26},{12,28},{14,30},{16,32}... | collective-permute-start | bytes 393224 | tf_op jit(solution)/shard_map/ppermute | solution.py:10
  132.8 30.5 %collective-permute-start.11 = (f32[1,128,256]{2,1,0:T(8,128)S(1)}, f32[1,128,256]{2,1,0:T(8,128)S(1)}, u32[]{:S(2)}, u32[]{:S(2)}) collective-permute-start(f32[1,128,256]{2,1,0:T(8,128)S(1)} %bitcast.672), channel_id=1, source_target_pairs={{0,32},{2,34},{4,36},{6,38},{8,40},{10,42},{12,44},{14,46},{16,48}... | collective-permute-start | bytes 393224 | tf_op jit(solution)/shard_map/ppermute | solution.py:10
  138.2 23.0 %collective-permute-start.19 = (f32[1,128]{1,0:T(1,128)S(1)}, f32[1,128]{1,0:T(1,128)S(1)}, u32[]{:S(2)}, u32[]{:S(2)}) collective-permute-start(f32[1,128]{1,0:T(1,128)S(1)} %bitcast.705), channel_id=1, source_target_pairs={{0,64},{2,66},{4,68},{6,70},{8,72},{10,74},{12,76},{14,78},{16,80}... | collective-permute-start | bytes 1544 | tf_op jit(solution)/shard_map/ppermute | solution.py:10
  145.1 37.6 %collective-permute-start.4 = (f32[1,128,256]{2,1,0:T(8,128)S(1)}, f32[1,128,256]{2,1,0:T(8,128)S(1)}, u32[]{:S(2)}, u32[]{:S(2)}) collective-permute-start(f32[1,128,256]{2,1,0:T(8,128)S(1)} %bitcast.665), channel_id=1, source_target_pairs={{32,0},{34,2},{36,4},{38,6},{40,8},{42,10},{44,12},{46,14},{48,16}... | collective-permute-start | bytes 393224 | tf_op jit(solution)/shard_map/ppermute | solution.py:10
  153.0 25.0 %collective-permute-start.36 = (f32[1,128,256]{2,1,0:T(8,128)S(1)}, f32[1,128,256]{2,1,0:T(8,128)S(1)}, u32[]{:S(2)}, u32[]{:S(2)}) collective-permute-start(f32[1,128,256]{2,1,0:T(8,128)S(1)} %bitcast.682), channel_id=1, source_target_pairs={{0,32},{2,34},{4,36},{6,38},{8,40},{10,42},{12,44},{14,46},{16,48}... | collective-permute-start | bytes 393224 | tf_op jit(solution)/shard_map/ppermute | solution.py:10
  165.6 23.4 %collective-permute-start.12 = (f32[1,128,256]{2,1,0:T(8,128)S(1)}, f32[1,128,256]{2,1,0:T(8,128)S(1)}, u32[]{:S(2)}, u32[]{:S(2)}) collective-permute-start(f32[1,128,256]{2,1,0:T(8,128)S(1)} %bitcast.673), channel_id=1, source_target_pairs={{0,64},{2,66},{4,68},{6,70},{8,72},{10,74},{12,76},{14,78},{16,80}... | collective-permute-start | bytes 393224 | tf_op jit(solution)/shard_map/ppermute | solution.py:10
  217.6 22.9 %collective-permute-start.39 = (f32[1,128,256]{2,1,0:T(8,128)S(1)}, f32[1,128,256]{2,1,0:T(8,128)S(1)}, u32[]{:S(2)}, u32[]{:S(2)}) collective-permute-start(f32[1,128,256]{2,1,0:T(8,128)S(1)} %bitcast.685), channel_id=1, source_target_pairs={{0,256},{2,258},{4,260},{6,262},{8,264},{10,266},{12,268},{14,270}... | collective-permute-start | bytes 393224 | tf_op jit(solution)/shard_map/ppermute | solution.py:10
  299.9 18.5 %collective-permute-start.6 = (f32[1,128,256]{2,1,0:T(8,128)S(1)}, f32[1,128,256]{2,1,0:T(8,128)S(1)}, u32[]{:S(2)}, u32[]{:S(2)}) collective-permute-start(f32[1,128,256]{2,1,0:T(8,128)S(1)} %bitcast.667), channel_id=1, source_target_pairs={{128,0},{130,2},{132,4},{134,6},{136,8},{138,10},{140,12},{142,14}... | collective-permute-start | bytes 393224 | tf_op jit(solution)/shard_map/ppermute | solution.py:10
  355.6 21.8 %collective-permute-start.48 = (f32[1,128,256]{2,1,0:T(8,128)S(1)}, f32[1,128,256]{2,1,0:T(8,128)S(1)}, u32[]{:S(2)}, u32[]{:S(2)}) collective-permute-start(f32[1,128,256]{2,1,0:T(8,128)S(1)} %bitcast.687), channel_id=1, source_target_pairs={{256,0},{258,2},{260,4},{262,6},{264,8},{266,10},{268,12},{270,14}... | collective-permute-start | bytes 393224 | tf_op jit(solution)/shard_map/ppermute | solution.py:10
  (33 other events, 286.0 us)
where the time goes:
time: 397 us; the launch traced here: 392 us
  blocking collectives  159 us (40%)
  starting transfers between devices  145 us (37%)
  waiting for transfers between devices  56.1 us (14%)
  matrix products  26.2 us (7%)
    ppermute x50, starting transfers between devices, shifted(): return lax.ppermute(value, axis, pairs)  145 us
    ppermute x50, waiting for transfers between devices, shifted(): return lax.ppermute(value, axis, pairs)  56.1 us
    all_gather x16, blocking collectives, combine(): lax.all_gather(head_shift, 'col', axis=1, tiled=True)  37.5 us
    all_gather x16, blocking collectives, combine(): lax.all_gather(head_cov, 'col', axis=1, tiled=True)  36.7 us
    all_gather x14, blocking collectives, combine(): lax.all_gather(head_map, 'col', axis=1, tiled=True)  30.8 us
    all_gather x14, blocking collectives, combine(): lax.all_gather(tail_map, 'col', axis=1, tiled=True)  27.9 us
    dot_general x61, matrix products, product(): return jnp.matmul(left, right, precision=lax.Precision.HIGHEST)  21 us
  transfers between devices with their start and end apart: 50, of which 12 were waited for; matrix products, arithmetic and copies ran while one was open for 5% of the time, Pallas kernels for 0%

commit v1 on v0

v1 whole, which is shorter than its diff:
```python
import functools

import jax
import jax.numpy as jnp
from jax import lax
from jax.experimental import pallas as pl
from jax.experimental.pallas import tpu as pltpu
from jax.sharding import PartitionSpec as P

MESH = pl.DeviceIdType.MESH
F32 = jnp.float32
N = 256
H = 128


def grid_dims(steps):
    return {256: (4, 8, 8), 8: (2, 2, 2), 4: (2, 2, 1)}[steps]


def parts(a):
    hi = a.astype(jnp.bfloat16)
    lo = (a - hi.astype(F32)).astype(jnp.bfloat16)
    return hi, lo


def mm(a, b, nt=False):
    ah, al = parts(a)
    bh, bl = parts(b)
    dims = (((1,), (1 if nt else 0,)), ((), ()))
    dot = functools.partial(lax.dot_general, dimension_numbers=dims, preferred_element_type=F32)
    return dot(ah, bh) + (dot(ah, bl) + dot(al, bh))


def cong(f, s, c8):
    t = mm(jnp.concatenate([s, c8], 0), f, nt=True)
    return mm(f, t[:N]), t[N:]


def iota(shape, dim):
    return lax.broadcasted_iota(jnp.int32, shape, dim)


def pack(s):
    r, c = iota((H, H), 0), iota((H, H), 1)
    s00, s01, s11 = s[:H, :H], s[:H, H:], s[H:, H:]
    tri = jnp.where(r >= c, s00, s11)
    d11 = jnp.sum(jnp.where(r == c, s11, 0.0), axis=0, keepdims=True)
    fold = lambda m: jnp.concatenate([m[: H // 2], m[H // 2 :]], 1)
    return fold(s01), fold(tri), d11


def unpack(b0, b1, d11):
    r, c = iota((H, H), 0), iota((H, H), 1)
    unfold = lambda m: jnp.concatenate([m[:, :H], m[:, H:]], 0)
    s01, tri = unfold(b0), unfold(b1)
    trit = tri.T
    s00 = jnp.where(r >= c, tri, trit)
    s11 = jnp.where(r == c, d11, jnp.where(r < c, tri, trit))
    top = jnp.concatenate([s00, s01], 1)
    low = jnp.concatenate([s01.T, s11], 1)
    return jnp.concatenate([top, low], 0)


def vec_block(c8, d11):
    d8 = jnp.broadcast_to(jnp.concatenate([jnp.zeros((1, H), F32), d11], 1), (8, N))
    return jnp.where(iota((8, N), 0) == 0, c8, d8)


def rows8(v):
    return jnp.broadcast_to(v, (8, N))


def kernel(dims, obs_ref, mask_ref, fg_ref, sg_ref, a_ref, q_ref, r_ref, m0_ref, p0_ref,
           mean_ref, cov_ref,
           mb, gb, fi, si, ci, yb, yv, zb, zv, ex, by, byv, bz, bzv, gm, lm,
           cf, cs, cc, pf, ps, pc, qf, qs, qc, hx, wy, xa, xc, ca, cv, send_sem, recv_sem):
    nx, ny, nz = dims
    t = lax.axis_index("tm")
    c = lax.axis_index("col")
    o = 1 - c
    x = lax.rem(t, nx)
    y = lax.rem(t // nx, ny)
    z = t // (nx * ny)

    def at_x(d):
        return (t - x + lax.rem(x + d, nx), c)

    def at_y(d):
        return (t - y * nx + lax.rem(y + d, ny) * nx, c)

    def at_z(d):
        return (t - z * (nx * ny) + lax.rem(z + d, nz) * (nx * ny), c)

    sib = (t, o)
    rings = {"x": (at_x, x, nx), "y": (at_y, y, ny), "z": (at_z, z, nz)}

    def order(n):
        out = []
        for d in range(1, n // 2 + 1):
            out.append(d)
            if d != n - d:
                out.append(n - d)
        return out if n > 1 else []

    barrier = pltpu.get_barrier_semaphore()
    peers = [sib]
    for at, _, n in rings.values():
        peers += [at(d) for d in range(1, n)]
    for dev in peers:
        pl.semaphore_signal(barrier, inc=1, device_id=dev, device_id_type=MESH)

    count = [0]
    sent = []

    def slots(k):
        count[0] += k
        return count[0] - k

    def start(ref, sem, dev):
        cp = pltpu.make_async_remote_copy(
            src_ref=ref, dst_ref=ref, send_sem=send_sem.at[sem], recv_sem=recv_sem.at[sem],
            device_id=dev, device_id_type=MESH)
        cp.start()
        sent.append(cp)

    def arrived(ref, sem):
        pltpu.make_async_remote_copy(
            src_ref=ref, dst_ref=ref, send_sem=send_sem.at[sem], recv_sem=recv_sem.at[sem],
            device_id=sib, device_id_type=MESH).wait_recv()

    class Gather:
        def __init__(self, ring, buf):
            self.at, self.me, self.n = rings[ring]
            self.buf = buf
            self.s1, self.s2 = slots(self.n), slots(self.n)

        def source(self, d):
            return lax.rem(self.me + self.n - d, self.n)

        def send(self):
            for d in order(self.n):
                start(self.buf.at[self.me, c], self.s1 + d, self.at(d))

        def swap(self, d):
            if d:
                arrived(self.buf.at[self.source(d), c], self.s1 + d)
            start(self.buf.at[self.source(d), c], self.s2 + d, sib)

        def swapped(self, d):
            arrived(self.buf.at[self.source(d), o], self.s2 + d)

        def finish(self):
            for d in order(self.n):
                self.swap(d)
            for d in order(self.n):
                self.swapped(d)

    class SplitGather:
        def __init__(self, ring, buf, vec):
            self.at, self.me, self.n = rings[ring]
            self.buf, self.vec = buf, vec
            self.s1, self.s2, self.sv = slots(self.n), slots(self.n), slots(self.n)
            self.s3 = slots(self.n * nx)

        def source(self, d):
            return lax.rem(self.me + self.n - d, self.n)

        def send(self):
            for d in order(self.n):
                start(self.buf.at[self.me, c, x], self.s1 + d, self.at(d))
            for d in order(self.n):
                start(self.vec.at[self.me], self.sv + d, self.at(d))

        def forward(self):
            for d in order(self.n):
                k = self.source(d)
                arrived(self.buf.at[k, c, x], self.s1 + d)
                for e in order(nx):
                    start(self.buf.at[k, c, x], self.s3 + d * nx + e, at_x(e))

        def collect(self):
            for d in order(self.n):
                k = self.source(d)
                for e in order(nx):
                    arrived(self.buf.at[k, c, lax.rem(x + nx - e, nx)], self.s3 + d * nx + e)
                start(self.buf.at[k, c], self.s2 + d, sib)
            for d in order(self.n):
                arrived(self.vec.at[self.source(d)], self.sv + d)

        def swapped(self):
            for d in order(self.n):
                arrived(self.buf.at[self.source(d), o], self.s2 + d)

    pr = H // nx
    sr = H // 2 // nx

    def put_item(buf, vec, k, f, s, c8):
        b0, b1, d11 = pack(s)
        for h, blk in ((0, b0), (1, b1)):
            for q in range(nx):
                buf[k, h, q, :pr] = f[h * H + q * pr : h * H + (q + 1) * pr]
                buf[k, h, q, pr:] = blk[q * sr : (q + 1) * sr]
        vec[k] = vec_block(c8, d11)

    def get_item(buf, vec, k):
        f = jnp.concatenate([buf[k, h, q, :pr] for h in range(2) for q in range(nx)], 0)
        b = [jnp.concatenate([buf[k, h, q, pr:] for q in range(nx)], 0) for h in range(2)]
        v = vec[k]
        return f, unpack(b[0], b[1], v[1:2, H:]), rows8(v[0:1])

    def put_sym(buf, vec, k, s, c8):
        b0, b1, d11 = pack(s)
        for h, blk in ((0, b0), (1, b1)):
            for q in range(nx):
                buf[k, h, q] = blk[q * sr : (q + 1) * sr]
        vec[k] = vec_block(c8, d11)

    def get_sym(buf, vec, k):
        b = [jnp.concatenate([buf[k, h, q] for q in range(nx)], 0) for h in range(2)]
        v = vec[k]
        return unpack(b[0], b[1], v[1:2, H:]), rows8(v[0:1])

    def whole(buf, k):
        return jnp.concatenate([buf[k, 0, :H], buf[k, 1, :H]], 0)

    mask = mask_ref[...].astype(F32)
    mb[x, c, :H] = fg_ref[...] * mask
    mb[x, c, H:] = rows8(obs_ref[...])
    gb[x, c] = sg_ref[...]
    pl.semaphore_wait(barrier, len(peers))
    m_ag, g_ag = Gather("x", mb), Gather("x", gb)
    m_ag.swap(0)
    m_ag.send()
    g_ag.swap(0)
    g_ag.send()

    def step_item(d):
        k = m_ag.source(d)
        m = whole(mb, k)
        both = mm(m, jnp.concatenate([a_ref[...], q_ref[...]], 1))
        u = both[:, N:]
        v = u + m * r_ref[...] - q_ref[...]
        w = mm(jnp.concatenate([v, mb[k, c, H:]], 0), m, nt=True)
        fi[k] = a_ref[...] - both[:, :N]
        si[k] = q_ref[...] - u + w[:N]
        ci[k] = w[N:]

    m_ag.swapped(0)
    step_item(0)
    for d in order(nx):
        m_ag.swap(d)
        m_ag.swapped(d)
        step_item(d)

    eye = jnp.where(iota((N, N), 0) == iota((N, N), 1), 1.0, 0.0).astype(F32)
    zero8 = jnp.zeros((8, N), F32)
    pf[...] = eye
    ps[...] = jnp.zeros((N, N), F32)
    pc[...] = zero8
    cf[...] = fi[0]
    cs[...] = si[0]
    cc[...] = ci[0]

    def chain(steps, me, item, f_ref, s_ref, c_ref):
        def body(k, carry):
            @pl.when(me == k)
            def _():
                f_ref[...] = cf[...]
                s_ref[...] = cs[...]
                c_ref[...] = cc[...]

            f, s, c8 = item(k)
            ns, nc = cong(f, cs[...], cc[...])
            cf[...] = mm(f, cf[...])
            cs[...] = ns + s
            cc[...] = nc + c8
            return carry

        lax.fori_loop(1, steps, body, 0)

    chain(nx, x, lambda k: (fi[k], si[k], ci[k]), pf, ps, pc)

    y_ag = SplitGather("y", yb, yv)
    put_item(yb, yv, y, cf[...], cs[...], cc[...])
    y_ag.send()

    g_ag.swapped(0)
    g_ag.finish()
    hx[...] = whole(gb, nx - 1)
    cf[...] = whole(gb, nx - 1)

    def back_x(i, carry):
        k = nx - 2 - i
        cf[...] = mm(whole(gb, k), cf[...])

        @pl.when(x == k)
        def _():
            hx[...] = cf[...]

        return carry

    lax.fori_loop(0, nx - 1, back_x, 0)
    gm[y, 0] = cf[:H]
    gm[y, 1] = cf[H:]

    y_ag.forward()
    y_ag.collect()
    y_ag.swapped()
    qf[...] = eye
    qs[...] = jnp.zeros((N, N), F32)
    qc[...] = zero8
    f0, s0, c0 = get_item(yb, yv, 0)
    cf[...] = f0
    cs[...] = s0
    cc[...] = c0
    chain(ny, y, lambda k: get_item(yb, yv, k), qf, qs, qc)

    z_ag = SplitGather("z", zb, zv)
    put_item(zb, zv, z, cf[...], cs[...], cc[...])
    z_ag.send()
    gm_ag = Gather("y", gm)
    gm_ag.send()
    ns, nc = cong(pf[...], qs[...], qc[...])
    qf[...] = mm(pf[...], qf[...])
    qs[...] = ns + ps[...]
    qc[...] = nc + pc[...]
    z_ag.forward()
    z_ag.collect()
    z_ag.swapped()
    cs[...] = p0_ref[...]
    cc[...] = rows8(m0_ref[...])

    def carry_in(k, carry):
        f, s, c8 = get_item(zb, zv, k)
        ns, nc = cong(f, cs[...], cc[...])
        cs[...] = ns + s
        cc[...] = nc + c8
        return carry

    lax.fori_loop(0, z, carry_in, 0)
    p_prev, m_prev = cong(qf[...], cs[...], cc[...])
    p_prev = p_prev + qs[...]
    m_prev = m_prev + qc[...]

    pred, am = cong(a_ref[...], p_prev, m_prev)
    pred = pred + q_ref[...]
    m = whole(mb, x)
    w = mm(m, pred)
    v = w + m * r_ref[...] - pred
    ee = mm(jnp.concatenate([v, rows8(obs_ref[...]) - am], 0), m, nt=True)
    e_cov = ee[:N] - w
    e_vec = ee[N:]
    b0, b1, d11 = pack(e_cov)
    vb = vec_block(e_vec, d11)
    for h, blk in ((0, b0), (1, b1)):
        ex[x, h, : H // 2] = blk
        ex[x, h, H // 2 :] = vb
    ps[...] = pred
    pc[...] = am

    e_ag = Gather("x", ex)
    e_ag.send()
    gm_ag.finish()
    wy[...] = eye
    cf[...] = whole(gm, ny - 1)

    def back_y_map(i, carry):
        k = ny - 2 - i

        @pl.when(y == k)
        def _():
            wy[...] = cf[...]

        cf[...] = mm(whole(gm, k), cf[...])
        return carry

    lax.fori_loop(0, ny - 1, back_y_map, 0)
    lm[z, 0] = cf[:H]
    lm[z, 1] = cf[H:]
    lm_ag = Gather("z", lm)
    lm_ag.send()
    e_ag.finish()

    def get_e(k):
        vb = ex[k, c, H // 2 :]
        return unpack(ex[k, 0, : H // 2], ex[k, 1, : H // 2], vb[1:2, H:]), rows8(vb[0:1])

    s, c8 = get_e(nx - 1)
    xa[...] = s
    xc[...] = c8
    cs[...] = s
    cc[...] = c8

    def back_x_cov(i, carry):
        k = nx - 2 - i
        s, c8 = get_e(k)
        ns, nc = cong(whole(gb, k), cs[...], cc[...])
        cs[...] = ns + s
        cc[...] = nc + c8

        @pl.when(x == k)
        def _():
            xa[...] = cs[...]
            xc[...] = cc[...]

        return carry

    lax.fori_loop(0, nx - 1, back_x_cov, 0)

    by_ag = SplitGather("y", by, byv)
    put_sym(by, byv, y, cs[...], cc[...])
    by_ag.send()
    by_ag.forward()
    by_ag.collect()
    by_ag.swapped()
    s, c8 = get_sym(by, byv, ny - 1)
    cs[...] = s
    cc[...] = c8
    ca[...] = jnp.zeros((N, N), F32)
    cv[...] = zero8

    def back_y_cov(i, carry):
        k = ny - 2 - i

        @pl.when(y == k)
        def _():
            ca[...] = cs[...]
            cv[...] = cc[...]

        s, c8 = get_sym(by, byv, k)
        ns, nc = cong(whole(gm, k), cs[...], cc[...])
        cs[...] = ns + s
        cc[...] = nc + c8
        return carry

    lax.fori_loop(0, ny - 1, back_y_cov, 0)

    bz_ag = SplitGather("z", bz, bzv)
    put_sym(bz, bzv, z, cs[...], cc[...])
    bz_ag.send()
    lm_ag.finish()
    ns, nc = cong(hx[...], ca[...], cv[...])
    xa[...] = xa[...] + ns
    xc[...] = xc[...] + nc
    hx[...] = mm(hx[...], wy[...])
    bz_ag.forward()
    bz_ag.collect()
    bz_ag.swapped()
    cs[...] = jnp.zeros((N, N), F32)
    cc[...] = zero8

    def back_z_cov(i, carry):
        k = nz - 1 - i
        s, c8 = get_sym(bz, bzv, k)
        ns, nc = cong(whole(lm, k), cs[...], cc[...])
        cs[...] = ns + s
        cc[...] = nc + c8
        return carry

    lax.fori_loop(0, nz - 1 - z, back_z_cov, 0)
    ns, nc = cong(hx[...], cs[...], cc[...])
    xa[...] = xa[...] + ns + ps[...]
    xc[...] = xc[...] + nc + pc[...]

    cov_ref[...] = xa[pl.ds(pl.multiple_of(c * H, H), H)]
    mean_ref[...] = jnp.where(c == 0, xc[0:1, :H], xc[0:1, H:])
    for cp in sent:
        cp.wait_send()


def shards(steps, observations, sensor_mask, filter_gain, smoother_gain, dynamics, process_noise,
           sensor_noise, initial_mean, initial_cov):
    dims = grid_dims(steps)
    nx, ny, nz = dims
    mat = pltpu.VMEM((N, N), F32)
    vec = pltpu.VMEM((8, N), F32)
    buf = lambda *s: pltpu.VMEM(s + (N,), F32)
    n_sem = 3 * nx * 2 + (ny + nz) * 2 + 2 * (ny + nz) * (3 + nx)
    vmem = pl.BlockSpec(memory_space=pltpu.VMEM)
    mean, cov = pl.pallas_call(
        functools.partial(kernel, dims),
        out_shape=(jax.ShapeDtypeStruct((1, H), F32), jax.ShapeDtypeStruct((H, N), F32)),
        in_specs=[vmem] * 9,
        out_specs=(vmem, vmem),
        scratch_shapes=[
            buf(nx, 2, H + 8), buf(nx, 2, H),
            buf(nx, N), buf(nx, N), buf(nx, 8),
            buf(ny, 2, nx, (H + H // 2) // nx), buf(ny, 8),
            buf(nz, 2, nx, (H + H // 2) // nx), buf(nz, 8),
            buf(nx, 2, H // 2 + 8),
            buf(ny, 2, nx, H // 2 // nx), buf(ny, 8),
            buf(nz, 2, nx, H // 2 // nx), buf(nz, 8),
            buf(ny, 2, H), buf(nz, 2, H),
            mat, mat, vec, mat, mat, vec, mat, mat, vec, mat, mat, mat, vec, mat, vec,
            pltpu.SemaphoreType.DMA((n_sem,)), pltpu.SemaphoreType.DMA((n_sem,)),
        ],
        compiler_params=pltpu.CompilerParams(
            collective_id=0, has_side_effects=True, vmem_limit_bytes=48 << 20),
    )(observations[0], sensor_mask[0], filter_gain[0, 0], smoother_gain[0, 0], dynamics[0],
      process_noise[0], sensor_noise, initial_mean, initial_cov[0])
    return mean[None], cov[None, None]


def solution(mesh):
    return jax.shard_map(
        functools.partial(shards, mesh.shape["tm"]),
        mesh=mesh,
        in_specs=(
            P(None, "tm", None),
            P(None, "tm", None),
            P(None, "tm", "col", None),
            P(None, "tm", "col", None),
            P(),
            P(),
            P(),
            P(),
            P(),
        ),
        out_specs=(P(None, "tm", "col"), P(None, "tm", "col", None)),
        check_vma=False,
    )
```

time: 397 us -> 145 us (0.37); the launches traced: 392 us -> 145 us
  blocking collectives: 159 us -> 0 us
  starting transfers between devices: 145 us -> 0 us
  Pallas kernels: 0 us -> 138 us
  waiting for transfers between devices: 56.1 us -> 0 us
  matrix products: 26.2 us -> 0 us
  local copies, waits for them, and re-layouts: 1.64 us -> 6.52 us
    all_gather x72 -> x0, blocking collectives: 159 us -> none  [the longest x16 37.5 us: combine(): lax.all_gather(head_shift, 'col', axis=1, tiled=True)]
    ppermute x50 -> x0, starting transfers between devices: 145 us -> none  [shifted(): return lax.ppermute(value, axis, pairs)]
    pallas_call x0 -> x1, Pallas kernels: none -> 138 us  [shards(): pl.pallas_call(functools.partial(kernel, dims), out_shape=(jax.ShapeDtype...]
    ppermute x50 -> x0, waiting for transfers between devices: 56.1 us -> none  [shifted(): return lax.ppermute(value, axis, pairs)]
    dot_general x83 -> x0, matrix products: 26.2 us -> none  [the longest x61 21 us: product(): return jnp.matmul(left, right, precision=lax.Precision.HIGHEST)]
    unnamed x14 -> x20, local copies, waits for them, and re-layouts: 1.64 us -> 6.52 us
  transfers between devices with their start and end apart: 50 -> 0, of which waited for: 12 -> 0; matrix products, arithmetic and copies ran while one was open for 5% -> 0% of each run, Pallas kernels for 0% -> 0%
where the time goes in v1:
time: 145 us
  Pallas kernels  138 us (95%)
  local copies, waits for them, and re-layouts  6.52 us (4%)
    pallas_call x1, Pallas kernels, shards(): pl.pallas_call(functools.partial(kernel, dims), out_shape=(jax.ShapeDtype...  138 us
    unnamed x20, local copies, waits for them, and re-layouts  6.52 us

profile of v1, /device:TPU:1, one launch (start us, length us, event | category | flops | bytes accessed | tf_op | source)
XLA Modules:
  0.0 144.9 jit_solution(13072125875408543640)
XLA Ops:
  0.6 0.0 copy-start.8
  0.6 0.0 copy-start.6
  0.7 0.0 copy-start.7
  0.7 0.0 copy-start.5
  0.7 0.6 copy-done.8
  1.3 0.0 copy-done.6
  1.3 0.0 copy-done.7
  1.3 0.0 copy-done.5
  1.4 0.0 copy-start
  1.4 0.9 copy-done
  2.3 0.0 copy-start.1
  2.3 0.9 copy-done.1
  3.3 0.0 copy-start.2
  3.3 0.9 copy-done.2
  4.2 0.0 copy-start.3
  4.2 0.9 copy-done.3
  5.1 0.0 copy-start.4
  5.1 0.9 copy-done.4
  6.0 137.7 %shard_map.104 = (f32[1,128]{1,0:T(1,128)S(1)}, f32[128,256]{1,0:T(8,128)S(1)}) custom-call(f32[1,256]{1,0:T(1,128)S(1)} %bitcast.15, s32[1,256]{1,0:T(1,128)S(1)} %bitcast.16, f32[128,256]{1,0:T(8,128)S(1)} %bitcast.13, f32[128,256]{1,0:T(8,128)S(1)} %bitcast.14, f32[256,256]{1,0:T(8,128)S(1)} %bitcast.9, f32[256,256]{1,0:T(8,128)S(1)} %bitcast.10, ...), custom_call_target="tpu_custom_call" | custom-call | tf_op jit(solution)/shard_map/pallas_call | solution.py:480
  143.7 0.5 copy.13
  144.2 0.7 copy.14
Async XLA Ops:
  0.6 0.7 copy-start.8
  0.6 0.7 copy-start.6
  0.7 0.7 copy-start.7
  0.7 0.7 copy-start.5
  1.4 0.9 copy-start
  2.3 0.9 copy-start.1
  3.3 0.9 copy-start.2
  4.2 0.9 copy-start.3
  5.1 0.9 copy-start.4

commit v2 on v1

--- a/solution.py
+++ b/solution.py
@@ -70,10 +70,11 @@
     return jnp.broadcast_to(v, (8, N))
 
 
-def kernel(dims, obs_ref, mask_ref, fg_ref, sg_ref, a_ref, q_ref, r_ref, m0_ref, p0_ref,
+def kernel(dims, obs_ref, mask_ref, r_ref, m0_ref, fg_hbm, sg_hbm, a_hbm, q_hbm, p0_hbm,
            mean_ref, cov_ref,
-           mb, gb, fi, si, ci, yb, yv, zb, zv, ex, by, byv, bz, bzv, gm, lm,
-           cf, cs, cc, pf, ps, pc, qf, qs, qc, hx, wy, xa, xc, ca, cv, send_sem, recv_sem):
+           a_ref, q_ref, p0_ref, mb, gb, fi, si, ci, yb, yv, zb, zv, ex, by, byv, bz, bzv, sb, tb, jb, gm, lm,
+           cf, cs, cc, pf, ps, pc, qf, qs, qc, hx, wy, ly, xa, xc, ca, cv, uf, rf, uc,
+           send_sem, recv_sem, load_sem):
     nx, ny, nz = dims
     t = lax.axis_index("tm")
     c = lax.axis_index("col")
@@ -102,6 +103,11 @@
                 out.append(n - d)
         return out if n > 1 else []
 
+    def load(i, src, dst):
+        cp = pltpu.make_async_copy(src, dst, load_sem.at[i])
+        cp.start()
+        return cp
+
     barrier = pltpu.get_barrier_semaphore()
     peers = [sib]
     for at, _, n in rings.values():
@@ -109,6 +115,10 @@
     for dev in peers:
         pl.semaphore_signal(barrier, inc=1, device_id=dev, device_id_type=MESH)
 
+    fg_load = load(0, fg_hbm, mb.at[x, c, pl.ds(0, H)])
+    sg_load = load(1, sg_hbm, gb.at[x, c])
+    other_loads = [load(2, a_hbm, a_ref), load(3, q_hbm, q_ref), load(4, p0_hbm, p0_ref)]
+
     count = [0]
     sent = []
 
@@ -187,9 +197,12 @@
             for d in order(self.n):
                 arrived(self.vec.at[self.source(d)], self.sv + d)
 
+        def swapped_one(self, d):
+            arrived(self.buf.at[self.source(d), o], self.s2 + d)
+
         def swapped(self):
             for d in order(self.n):
-                arrived(self.buf.at[self.source(d), o], self.s2 + d)
+                self.swapped_one(d)
 
     pr = H // nx
     sr = H // 2 // nx
@@ -224,15 +237,13 @@
         return jnp.concatenate([buf[k, 0, :H], buf[k, 1, :H]], 0)
 
     mask = mask_ref[...].astype(F32)
-    mb[x, c, :H] = fg_ref[...] * mask
     mb[x, c, H:] = rows8(obs_ref[...])
-    gb[x, c] = sg_ref[...]
+    fg_load.wait()
+    mb[x, c, :H] = mb[x, c, :H] * mask
     pl.semaphore_wait(barrier, len(peers))
     m_ag, g_ag = Gather("x", mb), Gather("x", gb)
+    m_ag.send()
     m_ag.swap(0)
-    m_ag.send()
-    g_ag.swap(0)
-    g_ag.send()
 
     def step_item(d):
         k = m_ag.source(d)
@@ -245,10 +256,16 @@
         si[k] = q_ref[...] - u + w[:N]
         ci[k] = w[N:]
 
+    for cp in other_loads:
+        cp.wait()
     m_ag.swapped(0)
     step_item(0)
     for d in order(nx):
         m_ag.swap(d)
+        if d == order(nx)[-1]:
+            sg_load.wait()
+            g_ag.swap(0)
+            g_ag.send()
         m_ag.swapped(d)
         step_item(d)
 
@@ -304,27 +321,76 @@
     gm[y, 1] = cf[H:]
 
     y_ag.forward()
+    gm_ag = Gather("y", gm)
+    gm_ag.send()
     y_ag.collect()
     y_ag.swapped()
+
+    cf[...] = eye
+    cs[...] = jnp.zeros((N, N), F32)
+    cc[...] = zero8
+    rf[...] = eye
+    uf[...] = jnp.zeros((N, N), F32)
+    uc[...] = zero8
+
+    def add_term():
+        term = mm(jnp.concatenate([uf[...], uc[...]], 0), rf[...], nt=True)
+        cs[...] += term[:N]
+        cc[...] += term[N:]
+
+    def total_y(i, carry):
+        f, s, c8 = get_item(yb, yv, ny - 1 - i)
+        r = cf[...]
+        both = mm(r, jnp.concatenate([f, s], 1))
+        add_term()
+        rf[...] = r
+        uf[...] = both[:, N:]
+        uc[...] = c8
+        cf[...] = both[:, :N]
+        return carry
+
+    lax.fori_loop(0, ny, total_y, 0)
+    add_term()
+
+    z_ag = SplitGather("z", zb, zv)
+    put_item(zb, zv, z, cf[...], cs[...], cc[...])
+    z_ag.send()
+
     qf[...] = eye
     qs[...] = jnp.zeros((N, N), F32)
     qc[...] = zero8
-    f0, s0, c0 = get_item(yb, yv, 0)
-    cf[...] = f0
-    cs[...] = s0
-    cc[...] = c0
-    chain(ny, y, lambda k: get_item(yb, yv, k), qf, qs, qc)
-
-    z_ag = SplitGather("z", zb, zv)
-    put_item(zb, zv, z, cf[...], cs[...], cc[...])
-    z_ag.send()
-    gm_ag = Gather("y", gm)
-    gm_ag.send()
-    ns, nc = cong(pf[...], qs[...], qc[...])
-    qf[...] = mm(pf[...], qf[...])
-    qs[...] = ns + ps[...]
-    qc[...] = nc + pc[...]
+
+    def before(f, s, c8):
+        ns, nc = cong(f, qs[...], qc[...])
+        qf[...] = mm(f, qf[...])
+        qs[...] = ns + s
+        qc[...] = nc + c8
+
+    def before_y(k, carry):
+        before(*get_item(yb, yv, k))
+        return carry
+
+    lax.fori_loop(0, y, before_y, 0)
+    before(pf[...], ps[...], pc[...])
     z_ag.forward()
+
+    gm_ag.finish()
+    cf[...] = eye
+
+    def map_y(k, carry):
+        @pl.when(y == k)
+        def _():
+            ly[...] = cf[...]
+
+        cf[...] = mm(cf[...], whole(gm, k))
+        return carry
+
+    lax.fori_loop(0, ny, map_y, 0)
+    lm[z, 0] = cf[:H]
+    lm[z, 1] = cf[H:]
+    lm_ag = Gather("z", lm)
+    lm_ag.send()
+
     z_ag.collect()
     z_ag.swapped()
     cs[...] = p0_ref[...]
@@ -360,12 +426,10 @@
 
     e_ag = Gather("x", ex)
     e_ag.send()
-    gm_ag.finish()
-    wy[...] = eye
-    cf[...] = whole(gm, ny - 1)
+    cf[...] = eye
 
     def back_y_map(i, carry):
-        k = ny - 2 - i
+        k = ny - 1 - i
 
         @pl.when(y == k)
         def _():
@@ -375,10 +439,12 @@
         return carry
 
     lax.fori_loop(0, ny - 1, back_y_map, 0)
-    lm[z, 0] = cf[:H]
-    lm[z, 1] = cf[H:]
-    lm_ag = Gather("z", lm)
-    lm_ag.send()
+
+    @pl.when(y == 0)
+    def _():
+        wy[...] = cf[...]
+
+    rf[...] = mm(hx[...], wy[...])
     e_ag.finish()
 
     def get_e(k):
@@ -407,60 +473,71 @@
 
     lax.fori_loop(0, nx - 1, back_x_cov, 0)
 
+    ns, nc = cong(ly[...], cs[...], cc[...])
+    b0, b1, d11 = pack(ns)
+    for h, blk in ((0, b0), (1, b1)):
+        for q in range(nx):
+            tb[h, q] = blk[q * sr : (q + 1) * sr]
+    sb[y, :sr] = tb[c, x]
+    sb[y, sr:] = vec_block(nc, d11)
+    s_slots = slots(ny)
+    for d in order(ny):
+        start(sb.at[y], s_slots + d, at_y(d))
     by_ag = SplitGather("y", by, byv)
     put_sym(by, byv, y, cs[...], cc[...])
     by_ag.send()
+
+    lm_ag.finish()
+    cf[...] = rf[...]
+
+    def map_z(k, carry):
+        jb[k] = cf[...]
+        cf[...] = mm(cf[...], whole(lm, k))
+        return carry
+
+    lax.fori_loop(z + 1, nz, map_z, 0)
+
+    for d in order(ny):
+        arrived(sb.at[by_ag.source(d)], s_slots + d)
+    total = sb[0]
+    for k in range(1, ny):
+        total = total + sb[k]
+    bz_ag = SplitGather("z", bz, bzv)
+    bz[z, c, x] = total[:sr]
+    bzv[z] = total[sr:]
+    bz_ag.send()
+
     by_ag.forward()
     by_ag.collect()
+    bz_ag.forward()
     by_ag.swapped()
-    s, c8 = get_sym(by, byv, ny - 1)
-    cs[...] = s
-    cc[...] = c8
     ca[...] = jnp.zeros((N, N), F32)
     cv[...] = zero8
 
     def back_y_cov(i, carry):
-        k = ny - 2 - i
-
-        @pl.when(y == k)
-        def _():
-            ca[...] = cs[...]
-            cv[...] = cc[...]
-
+        k = ny - 1 - i
         s, c8 = get_sym(by, byv, k)
-        ns, nc = cong(whole(gm, k), cs[...], cc[...])
-        cs[...] = ns + s
-        cc[...] = nc + c8
-        return carry
-
-    lax.fori_loop(0, ny - 1, back_y_cov, 0)
-
-    bz_ag = SplitGather("z", bz, bzv)
-    put_sym(bz, bzv, z, cs[...], cc[...])
-    bz_ag.send()
-    lm_ag.finish()
+        ns, nc = cong(whole(gm, k), ca[...], cv[...])
+        ca[...] = ns + s
+        cv[...] = nc + c8
+        return carry
+
+    lax.fori_loop(0, ny - 1 - y, back_y_cov, 0)
     ns, nc = cong(hx[...], ca[...], cv[...])
-    xa[...] = xa[...] + ns
-    xc[...] = xc[...] + nc
-    hx[...] = mm(hx[...], wy[...])
-    bz_ag.forward()
-    bz_ag.collect()
-    bz_ag.swapped()
-    cs[...] = jnp.zeros((N, N), F32)
-    cc[...] = zero8
-
-    def back_z_cov(i, carry):
-        k = nz - 1 - i
-        s, c8 = get_sym(bz, bzv, k)
-        ns, nc = cong(whole(lm, k), cs[...], cc[...])
-        cs[...] = ns + s
-        cc[...] = nc + c8
-        return carry
-
-    lax.fori_loop(0, nz - 1 - z, back_z_cov, 0)
-    ns, nc = cong(hx[...], cs[...], cc[...])
     xa[...] = xa[...] + ns + ps[...]
     xc[...] = xc[...] + nc + pc[...]
+
+    bz_ag.collect()
+    for d in order(nz):
+        k = bz_ag.source(d)
+        bz_ag.swapped_one(d)
+
+        @pl.when(k > z)
+        def _():
+            s, c8 = get_sym(bz, bzv, k)
+            ns, nc = cong(jb[k], s, c8)
+            xa[...] += ns
+            xc[...] += nc
 
     cov_ref[...] = xa[pl.ds(pl.multiple_of(c * H, H), H)]
     mean_ref[...] = jnp.where(c == 0, xc[0:1, :H], xc[0:1, H:])
@@ -475,14 +552,17 @@
     mat = pltpu.VMEM((N, N), F32)
     vec = pltpu.VMEM((8, N), F32)
     buf = lambda *s: pltpu.VMEM(s + (N,), F32)
-    n_sem = 3 * nx * 2 + (ny + nz) * 2 + 2 * (ny + nz) * (3 + nx)
+    n_sem = 3 * nx * 2 + (ny + nz) * 2 + 2 * (ny + nz) * (3 + nx) + ny
     vmem = pl.BlockSpec(memory_space=pltpu.VMEM)
+    hbm = pl.BlockSpec(memory_space=pltpu.HBM)
+    sr = H // 2 // nx
     mean, cov = pl.pallas_call(
         functools.partial(kernel, dims),
         out_shape=(jax.ShapeDtypeStruct((1, H), F32), jax.ShapeDtypeStruct((H, N), F32)),
-        in_specs=[vmem] * 9,
+        in_specs=[vmem] * 4 + [hbm] * 5,
         out_specs=(vmem, vmem),
         scratch_shapes=[
+            mat, mat, mat,
             buf(nx, 2, H + 8), buf(nx, 2, H),
             buf(nx, N), buf(nx, N), buf(nx, 8),
             buf(ny, 2, nx, (H + H // 2) // nx), buf(ny, 8),
@@ -490,14 +570,16 @@
             buf(nx, 2, H // 2 + 8),
             buf(ny, 2, nx, H // 2 // nx), buf(ny, 8),
             buf(nz, 2, nx, H // 2 // nx), buf(nz, 8),
-            buf(ny, 2, H), buf(nz, 2, H),
-            mat, mat, vec, mat, mat, vec, mat, mat, vec, mat, mat, mat, vec, mat, vec,
+            buf(ny, sr + 8), buf(2, nx, sr), buf(nz, N), buf(ny, 2, H), buf(nz, 2, H),
+            mat, mat, vec, mat, mat, vec, mat, mat, vec, mat, mat, mat, mat, vec, mat, vec,
+            mat, mat, vec,
             pltpu.SemaphoreType.DMA((n_sem,)), pltpu.SemaphoreType.DMA((n_sem,)),
+            pltpu.SemaphoreType.DMA((5,)),
         ],
         compiler_params=pltpu.CompilerParams(
-            collective_id=0, has_side_effects=True, vmem_limit_bytes=48 << 20),
-    )(observations[0], sensor_mask[0], filter_gain[0, 0], smoother_gain[0, 0], dynamics[0],
-      process_noise[0], sensor_noise, initial_mean, initial_cov[0])
+            collective_id=0, has_side_effects=True, vmem_limit_bytes=60 << 20),
+    )(observations[0], sensor_mask[0], sensor_noise, initial_mean, filter_gain[0, 0],
+      smoother_gain[0, 0], dynamics[0], process_noise[0], initial_cov[0])
     return mean[None], cov[None, None]
 
 

time: 145 us -> 131 us (0.903)
  Pallas kernels: 138 us -> 128 us
  local copies, waits for them, and re-layouts: 6.52 us -> 2.72 us
    pallas_call x1, Pallas kernels: 138 us -> 128 us  [shards(): pl.pallas_call(functools.partial(kernel, dims), out_shape=(jax.ShapeDtype...]
    unnamed x20 -> x4, local copies, waits for them, and re-layouts: 6.52 us -> 2.72 us
where the time goes in v2:
time: 131 us
  Pallas kernels  128 us (98%)
  local copies, waits for them, and re-layouts  2.72 us (2%)
    pallas_call x1, Pallas kernels, shards(): pl.pallas_call(functools.partial(kernel, dims), out_shape=(jax.ShapeDtype...  128 us
    unnamed x4, local copies, waits for them, and re-layouts  2.72 us

profile of v2, /device:TPU:1, one launch (start us, length us, event | category | flops | bytes accessed | tf_op | source)
XLA Modules:
  0.0 130.9 jit_solution(13379873547147854183)
XLA Ops:
  0.6 127.6 %shard_map.104 = (f32[1,128]{1,0:T(1,128)}, f32[128,256]{1,0:T(8,128)}) custom-call(f32[1,256]{1,0:T(1,128)} %bitcast.15, s32[1,256]{1,0:T(1,128)} %bitcast.16, f32[1,256]{1,0:T(1,128)} %r_ref.1, f32[1,256]{1,0:T(1,128)} %m0_ref.1, f32[128,256]{1,0:T(8,128)} %bitcast.13, f32[128,256]{1,0:T(8,128)} %bitcast.14, f32[256,256]{1,0:T(8,128)} %bitcast.9, ...), custom_call_target="tpu_custom_call" | custom-call | tf_op jit(solution)/shard_map/pallas_call | solution.py:559
  128.2 0.0 copy-start
  128.2 0.6 copy-done
  128.9 0.5 copy.13
  129.4 1.6 %copy.14 = f32[1,1,128,256]{3,2,1,0:T(8,128)} copy(f32[1,1,128,256]{3,2,1,0:T(8,128)} %bitcast.12) | data formatting | bytes 262144
Async XLA Ops:
  128.2 0.7 copy-start

commit v3 on v2

--- a/solution.py
+++ b/solution.py
@@ -73,7 +73,7 @@
 def kernel(dims, obs_ref, mask_ref, r_ref, m0_ref, fg_hbm, sg_hbm, a_hbm, q_hbm, p0_hbm,
            mean_ref, cov_ref,
            a_ref, q_ref, p0_ref, mb, gb, fi, si, ci, yb, yv, zb, zv, ex, by, byv, bz, bzv, sb, tb, jb, gm, lm,
-           cf, cs, cc, pf, ps, pc, qf, qs, qc, hx, wy, ly, xa, xc, ca, cv, uf, rf, uc,
+           cf, cs, cc, pf, ps, pc, qf, qs, qc, hx, wy, ly, xa, xc, ca, cv, uf, rf, uc, fy, sy, fz, sz,
            send_sem, recv_sem, load_sem):
     nx, ny, nz = dims
     t = lax.axis_index("tm")
@@ -165,6 +165,42 @@
             for d in order(self.n):
                 self.swapped(d)
 
+    maybe_sent = []
+
+    def maybe_start(cond, ref, sem, dev):
+        def copy():
+            return pltpu.make_async_remote_copy(
+                src_ref=ref, dst_ref=ref, send_sem=send_sem.at[sem], recv_sem=recv_sem.at[sem],
+                device_id=dev, device_id_type=MESH)
+
+        @pl.when(cond)
+        def _():
+            copy().start()
+
+        maybe_sent.append((cond, copy))
+
+    class DownGather(Gather):
+        def wanted(self, d):
+            return (self.source(d) > self.me) & (self.source(d) < self.n - 1)
+
+        def send(self):
+            for d in order(self.n):
+                to = lax.rem(self.me + d, self.n)
+                cond = (to < self.me) & (self.me < self.n - 1)
+                maybe_start(cond, self.buf.at[self.me, c], self.s1 + d, self.at(d))
+
+        def finish(self):
+            for d in order(self.n):
+                @pl.when(self.wanted(d))
+                def _():
+                    arrived(self.buf.at[self.source(d), c], self.s1 + d)
+
+                maybe_start(self.wanted(d), self.buf.at[self.source(d), c], self.s2 + d, sib)
+            for d in order(self.n):
+                @pl.when(self.wanted(d))
+                def _():
+                    arrived(self.buf.at[self.source(d), o], self.s2 + d)
+
     class SplitGather:
         def __init__(self, ring, buf, vec):
             self.at, self.me, self.n = rings[ring]
@@ -188,14 +224,28 @@
                 for e in order(nx):
                     start(self.buf.at[k, c, x], self.s3 + d * nx + e, at_x(e))
 
+        def collect_one(self, d):
+            k = self.source(d)
+            for e in order(nx):
+                arrived(self.buf.at[k, c, lax.rem(x + nx - e, nx)], self.s3 + d * nx + e)
+            start(self.buf.at[k, c], self.s2 + d, sib)
+            arrived(self.vec.at[k], self.sv + d)
+
         def collect(self):
             for d in order(self.n):
-                k = self.source(d)
-                for e in order(nx):
-                    arrived(self.buf.at[k, c, lax.rem(x + nx - e, nx)], self.s3 + d * nx + e)
-                start(self.buf.at[k, c], self.s2 + d, sib)
-            for d in order(self.n):
-                arrived(self.vec.at[self.source(d)], self.sv + d)
+                self.collect_one(d)
+
+        def unpacked(self, f_ref, s_ref):
+            ds = order(self.n)
+            for i in range(len(ds) + 1):
+                if i < len(ds):
+                    self.collect_one(ds[i])
+                if i > 0:
+                    self.swapped_one(ds[i - 1])
+                    k = self.source(ds[i - 1])
+                    f, s, _ = get_item(self.buf, self.vec, k)
+                    f_ref[k] = f
+                    s_ref[k] = s
 
         def swapped_one(self, d):
             arrived(self.buf.at[self.source(d), o], self.s2 + d)
@@ -300,6 +350,8 @@
     y_ag = SplitGather("y", yb, yv)
     put_item(yb, yv, y, cf[...], cs[...], cc[...])
     y_ag.send()
+    fy[y] = cf[...]
+    sy[y] = cs[...]
 
     g_ag.swapped(0)
     g_ag.finish()
@@ -323,12 +375,11 @@
     y_ag.forward()
     gm_ag = Gather("y", gm)
     gm_ag.send()
-    y_ag.collect()
-    y_ag.swapped()
-
-    cf[...] = eye
-    cs[...] = jnp.zeros((N, N), F32)
-    cc[...] = zero8
+    y_ag.unpacked(fy, sy)
+
+    cf[...] = fy[ny - 1]
+    cs[...] = sy[ny - 1]
+    cc[...] = rows8(yv[ny - 1, 0:1])
     rf[...] = eye
     uf[...] = jnp.zeros((N, N), F32)
     uc[...] = zero8
@@ -339,17 +390,17 @@
         cc[...] += term[N:]
 
     def total_y(i, carry):
-        f, s, c8 = get_item(yb, yv, ny - 1 - i)
+        k = ny - 1 - i
         r = cf[...]
-        both = mm(r, jnp.concatenate([f, s], 1))
+        both = mm(r, jnp.concatenate([fy[k], sy[k]], 1))
         add_term()
         rf[...] = r
         uf[...] = both[:, N:]
-        uc[...] = c8
+        uc[...] = rows8(yv[k, 0:1])
         cf[...] = both[:, :N]
         return carry
 
-    lax.fori_loop(0, ny, total_y, 0)
+    lax.fori_loop(1, ny, total_y, 0)
     add_term()
 
     z_ag = SplitGather("z", zb, zv)
@@ -367,7 +418,7 @@
         qc[...] = nc + c8
 
     def before_y(k, carry):
-        before(*get_item(yb, yv, k))
+        before(fy[k], sy[k], rows8(yv[k, 0:1]))
         return carry
 
     lax.fori_loop(0, y, before_y, 0)
@@ -388,19 +439,17 @@
     lax.fori_loop(0, ny, map_y, 0)
     lm[z, 0] = cf[:H]
     lm[z, 1] = cf[H:]
-    lm_ag = Gather("z", lm)
+    lm_ag = DownGather("z", lm)
     lm_ag.send()
 
-    z_ag.collect()
-    z_ag.swapped()
+    z_ag.unpacked(fz, sz)
     cs[...] = p0_ref[...]
     cc[...] = rows8(m0_ref[...])
 
     def carry_in(k, carry):
-        f, s, c8 = get_item(zb, zv, k)
-        ns, nc = cong(f, cs[...], cc[...])
-        cs[...] = ns + s
-        cc[...] = nc + c8
+        ns, nc = cong(fz[k], cs[...], cc[...])
+        cs[...] = ns + sz[k]
+        cc[...] = nc + rows8(zv[k, 0:1])
         return carry
 
     lax.fori_loop(0, z, carry_in, 0)
@@ -492,7 +541,11 @@
 
     def map_z(k, carry):
         jb[k] = cf[...]
-        cf[...] = mm(cf[...], whole(lm, k))
+
+        @pl.when(k < nz - 1)
+        def _():
+            cf[...] = mm(cf[...], whole(lm, k))
+
         return carry
 
     lax.fori_loop(z + 1, nz, map_z, 0)
@@ -543,6 +596,10 @@
     mean_ref[...] = jnp.where(c == 0, xc[0:1, :H], xc[0:1, H:])
     for cp in sent:
         cp.wait_send()
+    for cond, copy in maybe_sent:
+        @pl.when(cond)
+        def _():
+            copy().wait_send()
 
 
 def shards(steps, observations, sensor_mask, filter_gain, smoother_gain, dynamics, process_noise,
@@ -572,7 +629,7 @@
             buf(nz, 2, nx, H // 2 // nx), buf(nz, 8),
             buf(ny, sr + 8), buf(2, nx, sr), buf(nz, N), buf(ny, 2, H), buf(nz, 2, H),
             mat, mat, vec, mat, mat, vec, mat, mat, vec, mat, mat, mat, mat, vec, mat, vec,
-            mat, mat, vec,
+            mat, mat, vec, buf(ny, N), buf(ny, N), buf(nz, N), buf(nz, N),
             pltpu.SemaphoreType.DMA((n_sem,)), pltpu.SemaphoreType.DMA((n_sem,)),
             pltpu.SemaphoreType.DMA((5,)),
         ],

time: 131 us -> 131 us (level)
  no operation moved by 1% of the time
where the time goes in v3:
time: 131 us; the launch traced here: 130 us
  Pallas kernels  127 us (97%)
  local copies, waits for them, and re-layouts  2.72 us (2%)
    pallas_call x1, Pallas kernels, shards(): pl.pallas_call(functools.partial(kernel, dims), out_shape=(jax.ShapeDtype...  127 us
    unnamed x4, local copies, waits for them, and re-layouts  2.72 us

profile of v3, /device:TPU:1, one launch (start us, length us, event | category | flops | bytes accessed | tf_op | source)
XLA Modules:
  0.0 130.3 jit_solution(14683331208551409414)
XLA Ops:
  0.6 127.0 %shard_map.104 = (f32[1,128]{1,0:T(1,128)}, f32[128,256]{1,0:T(8,128)}) custom-call(f32[1,256]{1,0:T(1,128)} %bitcast.15, s32[1,256]{1,0:T(1,128)} %bitcast.16, f32[1,256]{1,0:T(1,128)} %r_ref.1, f32[1,256]{1,0:T(1,128)} %m0_ref.1, f32[128,256]{1,0:T(8,128)} %bitcast.13, f32[128,256]{1,0:T(8,128)} %bitcast.14, f32[256,256]{1,0:T(8,128)} %bitcast.9, ...), custom_call_target="tpu_custom_call" | custom-call | tf_op jit(solution)/shard_map/pallas_call | solution.py:616
  127.6 0.0 copy-start
  127.6 0.6 copy-done
  128.2 0.5 copy.13
  128.8 1.6 %copy.14 = f32[1,1,128,256]{3,2,1,0:T(8,128)} copy(f32[1,1,128,256]{3,2,1,0:T(8,128)} %bitcast.12) | data formatting | bytes 262144
Async XLA Ops:
  127.6 0.7 copy-start

commit v4 on v3

--- a/solution.py
+++ b/solution.py
@@ -221,7 +221,7 @@
             for d in order(self.n):
                 k = self.source(d)
                 arrived(self.buf.at[k, c, x], self.s1 + d)
-                for e in order(nx):
+                for e in order(nx)[::-1]:
                     start(self.buf.at[k, c, x], self.s3 + d * nx + e, at_x(e))
 
         def collect_one(self, d):

time: 131 us -> 131 us (level)
  no operation moved by 1% of the time
where the time goes in v4:
time: 131 us
  Pallas kernels  127 us (97%)
  local copies, waits for them, and re-layouts  2.72 us (2%)
    pallas_call x1, Pallas kernels, shards(): pl.pallas_call(functools.partial(kernel, dims), out_shape=(jax.ShapeDtype...  127 us
    unnamed x4, local copies, waits for them, and re-layouts  2.72 us

profile of v4, /device:TPU:1, one launch (start us, length us, event | category | flops | bytes accessed | tf_op | source)
XLA Modules:
  0.0 130.5 jit_solution(15816183905251457434)
XLA Ops:
  0.6 127.2 %shard_map.104 = (f32[1,128]{1,0:T(1,128)}, f32[128,256]{1,0:T(8,128)}) custom-call(f32[1,256]{1,0:T(1,128)} %bitcast.15, s32[1,256]{1,0:T(1,128)} %bitcast.16, f32[1,256]{1,0:T(1,128)} %r_ref.1, f32[1,256]{1,0:T(1,128)} %m0_ref.1, f32[128,256]{1,0:T(8,128)} %bitcast.13, f32[128,256]{1,0:T(8,128)} %bitcast.14, f32[256,256]{1,0:T(8,128)} %bitcast.9, ...), custom_call_target="tpu_custom_call" | custom-call | tf_op jit(solution)/shard_map/pallas_call | solution.py:616
  127.8 0.0 copy-start
  127.8 0.6 copy-done
  128.5 0.5 copy.13
  129.0 1.6 %copy.14 = f32[1,1,128,256]{3,2,1,0:T(8,128)} copy(f32[1,1,128,256]{3,2,1,0:T(8,128)} %bitcast.12) | data formatting | bytes 262144
Async XLA Ops:
  127.8 0.7 copy-start
